TPU v7x, 128 devices: a whole 4x4x4 slice. The times are simulated.
128 devices in a mesh: row: 16 (over y, z_hi, core), col: 8 (over x, z_lo).
Axes of the slice: x: 4, y: 4, z: 4 (z_hi: 2, z_lo: 2; z = z_hi * 2 + z_lo), core: 2. Of those that a mesh axis runs over, the one named last changes fastest.
Arguments:
- front: float32 [16384, 16384], P('row', 'col'), may hold values from -6 to 6
- child_upd: bfloat16 [16384, 8192], P('row', 'col'), may hold values from -6 to 6
- child_map: int32 [2, 64], replicated, may hold values from 0 to 127, as said below
- diag_inv: float32 [4, 128, 128], replicated, may hold values from -0.1875 to 0.1875
Outputs:
- factored: float32 [16384, 16384], P('row', 'col')
- panels: bfloat16 [16384, 512], P('row')
Inputs may be any that keep to these rules, and one draw needn't show every extreme that they name: `child_map`: within each child the 64 entries are distinct. Each aligned group of 8 consecutive entries of one child holds every residue modulo 8 exactly once, hence distinct residues modulo 16 too.
All inputs are finite; a program needn't handle non-finite values.
Results may differ from a plain program's by a relative error of at most 0.0039.
Values may be sent and summed in bfloat16 or wider, within the bound.
A program may use at most 128 MiB of HBM per device.

v0:
```python
import jax
import jax.numpy as jnp
from jax import lax
from jax.sharding import PartitionSpec as P


def broadcast(block, axis, source):
    block = jnp.where(lax.axis_index(axis) == source, block, jnp.zeros_like(block))
    return lax.psum(block, axis)


def outer_update(rows_panel, cols_panel):
    return lax.dot_general(
        rows_panel, cols_panel, (((1,), (1,)), ((), ())), preferred_element_type=jnp.float32
    )


def make_panel(column, diag_block, panel_idx, row_glob, block_size, my_col, col_count, row_count):
    candidate = jnp.dot(
        column, diag_block.T, precision=lax.Precision.HIGHEST, preferred_element_type=jnp.float32
    )
    keep_rows = jnp.repeat(row_glob > panel_idx, block_size)
    candidate = jnp.where(keep_rows[:, None], candidate, jnp.zeros_like(candidate)).astype(
        jnp.bfloat16
    )
    rows_panel = broadcast(candidate, "col", panel_idx % col_count)
    row_blocks = rows_panel.shape[0] // block_size
    copies = [
        broadcast(rows_panel, "row", my_col + copy_idx * col_count)
        for copy_idx in range(row_count // col_count)
    ]
    stacked = jnp.stack(
        [copy_part.reshape(row_blocks, block_size, block_size) for copy_part in copies], axis=1
    )
    return (rows_panel, stacked.reshape(-1, block_size))


def on_device(front, child_upd, child_map, diag_inv):
    row_count = lax.axis_size("row")
    col_count = lax.axis_size("col")
    my_row = lax.axis_index("row")
    my_col = lax.axis_index("col")
    block_size = diag_inv.shape[1]
    panel_count = diag_inv.shape[0]
    row_blocks = front.shape[0] // block_size
    col_blocks = front.shape[1] // block_size
    updates = child_upd.reshape(row_blocks, block_size, row_blocks, block_size).transpose(
        0, 2, 1, 3
    )
    groups = child_map.reshape(row_count, row_blocks)
    col_groups = child_map.reshape(2, col_count, row_blocks)
    own_rows = lax.dynamic_index_in_dim(groups, my_row, 0, keepdims=False)
    child_cols = lax.dynamic_index_in_dim(col_groups, my_row // col_count, 0, keepdims=False)
    own_cols = lax.dynamic_index_in_dim(child_cols, my_col, 0, keepdims=False)
    row_hit = (own_rows % row_count)[None, :] == jnp.arange(row_count)[:, None]
    source_row = jnp.sum(jnp.where(row_hit, jnp.arange(row_blocks)[None, :], 0), axis=1)
    row_present = jnp.any(row_hit, axis=1)
    col_hit = (own_cols % col_count)[None, :] == jnp.arange(col_count)[:, None]
    source_col = jnp.sum(jnp.where(col_hit, jnp.arange(row_blocks)[None, :], 0), axis=1)
    outgoing = jnp.take(jnp.take(updates, source_row, axis=0), source_col, axis=1)
    outgoing = jnp.where(row_present[:, None, None, None], outgoing, jnp.zeros_like(outgoing))
    flat = outgoing.reshape(row_count * col_count, block_size, block_size)
    received = lax.all_to_all(
        flat, ("row", "col"), split_axis=0, concat_axis=0, tiled=True
    ).reshape(row_count, col_count, block_size, block_size)
    all_hit = groups % row_count == my_row
    recv_present = jnp.any(all_hit, axis=1)
    recv_slot = jnp.sum(jnp.where(all_hit, groups // row_count, 0), axis=1)
    row_weight = (
        (recv_slot[None, :] == jnp.arange(row_blocks)[:, None]) & recv_present[None, :]
    ).astype(jnp.bfloat16)
    recv_col_hit = col_groups % col_count == my_col
    recv_col_slot = jnp.sum(jnp.where(recv_col_hit, col_groups // col_count, 0), axis=2)
    col_weight = (recv_col_slot[:, None, :] == jnp.arange(col_blocks)[None, :, None]).astype(
        jnp.bfloat16
    )
    added = jnp.zeros((row_blocks, block_size, col_blocks, block_size), jnp.float32)
    for child_idx in range(2):
        child_part = received[child_idx * col_count : (child_idx + 1) * col_count]
        child_rows = row_weight[:, child_idx * col_count : (child_idx + 1) * col_count]
        placed_rows = jnp.einsum(
            "lx,xyab->lyab", child_rows, child_part, preferred_element_type=jnp.float32
        ).astype(jnp.bfloat16)
        added = added + jnp.einsum(
            "lyab,my->lamb", placed_rows, col_weight[child_idx], preferred_element_type=jnp.float32
        )
    front_now = front + added.reshape(row_blocks * block_size, col_blocks * block_size)
    row_glob = jnp.arange(row_blocks, dtype=jnp.int32) * row_count + my_row
    panels_out = jnp.zeros((row_blocks * block_size, panel_count * block_size), jnp.bfloat16)

    def column_of(front_now, panel_idx):
        return lax.dynamic_slice_in_dim(
            front_now, panel_idx // col_count * block_size, block_size, 1
        )

    def panel_from(column, panel_idx):
        diag_block = lax.dynamic_index_in_dim(diag_inv, panel_idx, 0, keepdims=False)
        return make_panel(
            column, diag_block, panel_idx, row_glob, block_size, my_col, col_count, row_count
        )

    def plain_step(panel_idx, carry):
        front_now, panels_out = carry
        rows_panel, cols_panel = panel_from(column_of(front_now, panel_idx), panel_idx)
        panels_out = lax.dynamic_update_slice_in_dim(
            panels_out, rows_panel, panel_idx * block_size, 1
        )
        front_now = front_now - outer_update(rows_panel, cols_panel)
        return (front_now, panels_out)

    front_now, panels_out = lax.fori_loop(0, panel_count, plain_step, (front_now, panels_out))
    return (front_now, panels_out)


def solution(mesh):
    return jax.shard_map(
        on_device,
        mesh=mesh,
        in_specs=(P("row", "col"), P("row", "col"), P(), P()),
        out_specs=(P("row", "col"), P("row", None)),
        check_vma=False,
    )
```

profile of v0, /device:TPU:1, one launch (start us, length us, event | category | flops | bytes accessed | tf_op | source)
XLA Modules:
  0.0 1041.8 jit_solution(5950990180659108426)
XLA Ops:
  7.2 0.8 reshape.121
  7.9 0.1 select_reduce_fusion
  8.1 0.1 fusion.28
  8.2 0.8 reshape.120
  9.0 0.1 select_reduce_fusion.1
  9.1 0.1 broadcast_in_dim.116
  9.2 0.1 broadcast_in_dim.117
  9.3 0.1 broadcast_in_dim.122
  9.4 2.2 copy.34
  11.6 0.6 copy.50
  12.2 3.1 gather_fusion
  15.3 4.7 broadcast_select_fusion.2
  20.0 5.2 gather_fusion.1
  25.2 2.5 copy.25
  27.7 2.8 fusion.8
  30.5 12.0 %all-to-all-start = ((bf16[128,128,128]{2,1,0:T(8,128)(2,1)}), bf16[128,128,128]{2,1,0:T(8,128)(2,1)}, u32[]{:S(2)}, u32[]{:S(2)}) async-start(bf16[128,128,128]{2,1,0:T(8,128)(2,1)} %fusion.8), calls=%async_computation | async-start | bytes 8388608 | tf_op jit(solution)/shard_map/all_to_all | solution.py:63
  42.5 0.1 fusion.43
  42.6 0.1 fusion.27
  42.7 0.2 fusion.24
  42.9 0.1 iota_compare_fusion.1
  43.0 51.3 %all-to-all-done = bf16[128,128,128]{2,1,0:T(8,128)(2,1)} async-done(((bf16[128,128,128]{2,1,0:T(8,128)(2,1)}), bf16[128,128,128]{2,1,0:T(8,128)(2,1)}, u32[]{:S(2)}, u32[]{:S(2)}) %all-to-all-start) | async-done | bytes 4194336 | tf_op jit(solution)/shard_map/all_to_all | solution.py:63
  94.3 2.7 fusion.45
  97.0 1.3 fusion.19
  98.4 1.3 fusion.16
  99.7 2.6 fusion.12
  102.2 5.2 convolution_add_fusion
  107.4 13.9 %bitcast_add_fusion = f32[1024,2048]{1,0:T(8,128)} fusion(f32[1024,2048]{1,0:T(8,128)} %param.6, f32[128,8,16,128]{3,2,1,0:T(8,128)} %bitcast.83), kind=kLoop, calls=%fused_computation.17 | loop fusion | flops 2097152 | bytes 25165824 | tf_op jit(solution)/shard_map/add | solution.py:87
  121.3 0.1 broadcast_in_dim.129
  121.4 912.6 %while.18 = (s32[]{:T(128)}, f32[1024,2048]{1,0:T(8,128)}, bf16[1024,512]{1,0:T(8,128)(2,1)S(1)}, f32[4,128,128]{2,1,0:T(8,128)}, s32[]{:T(128)}, /*index=5*/s32...) while((s32[]{:T(128)}, f32[1024,2048]{1,0:T(8,128)}, ...), condition=%wide.region_10.11_spmd.clone, body=%wide.region_6.10_spmd.clone.sunk | while | flops 741605440 | bytes 25234492 | solution.py:111
  121.4 0.0 all-reduce.6.cloned.1.call-start
  121.5 0.1 broadcast_bitcast_fusion.2
  121.6 2.3 fusion.57
  123.9 0.0 all-reduce.6.cloned.1.call-update
  123.9 0.0 all-reduce.8.cloned.1.call-start
  124.0 67.3 %all-reduce.6.cloned.1.call-done = bf16[1024,128]{1,0:T(8,128)(2,1)} async-done(((bf16[1024,128]{1,0:T(8,128)(2,1)}), bf16[1024,128]{1,0:T(8,128)(2,1)}) %all-reduce.6.cloned.1.call-update) | async-done | bytes 262160 | tf_op jit(solution)/shard_map/while/body/eval_jaxpr/psum | solution.py:9
  191.3 1.9 constant_dynamic-update-slice_fusion.2
  193.3 144.5 %all-reduce.8.cloned.1.call-done = (bf16[8,1,128,128]{3,2,1,0:T(8,128)(2,1)}, bf16[8,1,128,128]{3,2,1,0:T(8,128)(2,1)}) async-done(((bf16[8,1,128,128]{3,2,1,0:T(8,128)(2,1)}, bf16[8,1,128,128]{3,2,1,0:T(8,128)(2,1)}), (bf16[8,1,128,128]{3,2,1,0:T(8,128)(2,1)}, bf16[8,1,128,128]{3,2,1,0:T(8,128)(2,1)})) %all-reduce.8.cloned.1.call-update) | async-done | bytes 524304 | tf_op jit(solution)/shard_map/while/body/eval_jaxpr/psum | solution.py:9
  337.7 1.1 pad_maximum_fusion.2
  338.8 8.1 convolution_subtract_fusion.2
  347.0 0.1 broadcast_bitcast_fusion.2
  347.1 2.3 fusion.57
  349.4 0.0 all-reduce.8.cloned.1.call-start
  349.5 70.9 %all-reduce.6.cloned.1.call-done = bf16[1024,128]{1,0:T(8,128)(2,1)} async-done(((bf16[1024,128]{1,0:T(8,128)(2,1)}), bf16[1024,128]{1,0:T(8,128)(2,1)}) %all-reduce.6.cloned.1.call-update) | async-done | bytes 262160 | tf_op jit(solution)/shard_map/while/body/eval_jaxpr/psum | solution.py:9
  420.4 1.9 constant_dynamic-update-slice_fusion.2
  422.3 144.6 %all-reduce.8.cloned.1.call-done = (bf16[8,1,128,128]{3,2,1,0:T(8,128)(2,1)}, bf16[8,1,128,128]{3,2,1,0:T(8,128)(2,1)}) async-done(((bf16[8,1,128,128]{3,2,1,0:T(8,128)(2,1)}, bf16[8,1,128,128]{3,2,1,0:T(8,128)(2,1)}), (bf16[8,1,128,128]{3,2,1,0:T(8,128)(2,1)}, bf16[8,1,128,128]{3,2,1,0:T(8,128)(2,1)})) %all-reduce.8.cloned.1.call-update) | async-done | bytes 524304 | tf_op jit(solution)/shard_map/while/body/eval_jaxpr/psum | solution.py:9
  566.9 1.1 pad_maximum_fusion.2
  568.0 8.1 convolution_subtract_fusion.2
  576.1 0.1 broadcast_bitcast_fusion.2
  576.2 2.3 fusion.57
  578.6 0.0 all-reduce.8.cloned.1.call-start
  578.7 70.6 %all-reduce.6.cloned.1.call-done = bf16[1024,128]{1,0:T(8,128)(2,1)} async-done(((bf16[1024,128]{1,0:T(8,128)(2,1)}), bf16[1024,128]{1,0:T(8,128)(2,1)}) %all-reduce.6.cloned.1.call-update) | async-done | bytes 262160 | tf_op jit(solution)/shard_map/while/body/eval_jaxpr/psum | solution.py:9
  649.2 1.9 constant_dynamic-update-slice_fusion.2
  651.1 144.6 %all-reduce.8.cloned.1.call-done = (bf16[8,1,128,128]{3,2,1,0:T(8,128)(2,1)}, bf16[8,1,128,128]{3,2,1,0:T(8,128)(2,1)}) async-done(((bf16[8,1,128,128]{3,2,1,0:T(8,128)(2,1)}, bf16[8,1,128,128]{3,2,1,0:T(8,128)(2,1)}), (bf16[8,1,128,128]{3,2,1,0:T(8,128)(2,1)}, bf16[8,1,128,128]{3,2,1,0:T(8,128)(2,1)})) %all-reduce.8.cloned.1.call-update) | async-done | bytes 524304 | tf_op jit(solution)/shard_map/while/body/eval_jaxpr/psum | solution.py:9
  795.7 1.1 pad_maximum_fusion.2
  796.8 8.1 convolution_subtract_fusion.2
  804.9 0.1 broadcast_bitcast_fusion.2
  805.0 2.3 fusion.57
  807.4 0.0 all-reduce.8.cloned.1.call-start
  807.5 70.9 %all-reduce.6.cloned.1.call-done = bf16[1024,128]{1,0:T(8,128)(2,1)} async-done(((bf16[1024,128]{1,0:T(8,128)(2,1)}), bf16[1024,128]{1,0:T(8,128)(2,1)}) %all-reduce.6.cloned.1.call-update) | async-done | bytes 262160 | tf_op jit(solution)/shard_map/while/body/eval_jaxpr/psum | solution.py:9
  878.4 1.9 constant_dynamic-update-slice_fusion.2
  880.3 144.5 %all-reduce.8.cloned.1.call-done = (bf16[8,1,128,128]{3,2,1,0:T(8,128)(2,1)}, bf16[8,1,128,128]{3,2,1,0:T(8,128)(2,1)}) async-done(((bf16[8,1,128,128]{3,2,1,0:T(8,128)(2,1)}, bf16[8,1,128,128]{3,2,1,0:T(8,128)(2,1)}), (bf16[8,1,128,128]{3,2,1,0:T(8,128)(2,1)}, bf16[8,1,128,128]{3,2,1,0:T(8,128)(2,1)})) %all-reduce.8.cloned.1.call-update) | async-done | bytes 524304 | tf_op jit(solution)/shard_map/while/body/eval_jaxpr/psum | solution.py:9
  1024.8 1.1 pad_maximum_fusion.2
  1025.9 8.1 convolution_subtract_fusion.2
  1034.0 1.0 copy-done
  (25 shorter events, 0.2 us)
Async XLA Ops:
  30.5 63.8 %all-to-all-start = ((bf16[128,128,128]{2,1,0:T(8,128)(2,1)}), bf16[128,128,128]{2,1,0:T(8,128)(2,1)}, u32[]{:S(2)}, u32[]{:S(2)}) async-start(bf16[128,128,128]{2,1,0:T(8,128)(2,1)} %fusion.8), calls=%async_computation | async-start | bytes 8388608 | tf_op jit(solution)/shard_map/all_to_all | solution.py:63
  121.4 69.9 %all-reduce.6.cloned.1.call-start = ((), (), s32[]{:S(2)}) async-start(), calls=%async_computation.1 | async-start | bytes 524288 | tf_op jit(solution)/shard_map/while/body/eval_jaxpr/psum | solution.py:9
  123.9 213.8 %all-reduce.8.cloned.1.call-start = ((), (), s32[]{:S(2)}) async-start(), calls=%async_computation.2 | async-start | bytes 1048576 | tf_op jit(solution)/shard_map/while/body/eval_jaxpr/psum | solution.py:9
  347.0 73.4 %all-reduce.6.cloned.1.call-start = ((), (), s32[]{:S(2)}) async-start(), calls=%async_computation.1 | async-start | bytes 524288 | tf_op jit(solution)/shard_map/while/body/eval_jaxpr/psum | solution.py:9
  349.4 217.5 %all-reduce.8.cloned.1.call-start = ((), (), s32[]{:S(2)}) async-start(), calls=%async_computation.2 | async-start | bytes 1048576 | tf_op jit(solution)/shard_map/while/body/eval_jaxpr/psum | solution.py:9
  576.1 73.1 %all-reduce.6.cloned.1.call-start = ((), (), s32[]{:S(2)}) async-start(), calls=%async_computation.1 | async-start | bytes 524288 | tf_op jit(solution)/shard_map/while/body/eval_jaxpr/psum | solution.py:9
  578.6 217.1 %all-reduce.8.cloned.1.call-start = ((), (), s32[]{:S(2)}) async-start(), calls=%async_computation.2 | async-start | bytes 1048576 | tf_op jit(solution)/shard_map/while/body/eval_jaxpr/psum | solution.py:9
  804.9 73.4 %all-reduce.6.cloned.1.call-start = ((), (), s32[]{:S(2)}) async-start(), calls=%async_computation.1 | async-start | bytes 524288 | tf_op jit(solution)/shard_map/while/body/eval_jaxpr/psum | solution.py:9
  807.4 217.4 %all-reduce.8.cloned.1.call-start = ((), (), s32[]{:S(2)}) async-start(), calls=%async_computation.2 | async-start | bytes 1048576 | tf_op jit(solution)/shard_map/while/body/eval_jaxpr/psum | solution.py:9
  1034.0 1.0 copy-start
Sparse Core Ops, SparseCore 0:
  125.3 66.0 all-reduce.5
  194.6 143.1 all-reduce.7
  350.8 69.5 all-reduce.5
  423.5 143.3 all-reduce.7
  579.7 69.4 all-reduce.5
  652.3 143.3 all-reduce.7
  808.8 69.5 all-reduce.5
  881.6 143.1 all-reduce.7
where the time goes:
time: 1040 us
  waiting for transfers between devices  909 us (87%)
  matrix products  52.3 us (5%)
  other arithmetic  34.2 us (3%)
  local copies, waits for them, and re-layouts  19.4 us (2%)
  between operations  14.1 us (1%)
  starting transfers between devices  12.2 us (1%)
    psum x8, waiting for transfers between devices, broadcast(): return lax.psum(block, axis)  858 us
    all_to_all x1, waiting for transfers between devices, on_device(): lax.all_to_all(flat, ('row', 'col'), split_axis=0, concat_axis=0, tiled=T...  51.3 us
    dot_general x4, matrix products, outer_update(): lax.dot_general(rows_panel, cols_panel, (((1,), (1,)), ((), ())), preferr...  32.5 us
  transfers between devices with their start and end apart: 9, of which 9 were waited for; matrix products, arithmetic and copies ran while one was open for 0% of the time, Pallas kernels for 0%

commit v1 on v0

v1 whole, which is shorter than its diff:
```python
import jax
import jax.numpy as jnp
from jax import lax
from jax.experimental import pallas as pl
from jax.experimental.pallas import tpu as pltpu

MESH = pl.DeviceIdType.MESH
BLK = 128
HI = lax.Precision.HIGHEST
COL_STEPS = ((0, 1), (1, 0), (3, 0), (1, 1), (3, 1), (2, 0), (2, 1))
TOP_AT = (0, 0, 1, 3)


def exchange_kernel(
    cm, upd_hbm, front_hbm, dinv,
    r3, lr, lc, tab,
    upd, fcol, s1, r1, r2, wsel, rw, acol, ab, tp, tt, tf, lb, xa,
    load_sem, c_s, c_r, z_s, z_r, z_l, y_s, y_r, y_l, w_s, w_r, w_l,
    a_s, a_r, tp_s, tp_r, tb_s, tb_r, tc_s, tc_r,
    lr_s, lr_r, lr_l, al_s, al_r, be_s, be_r, be_l, fo_s, fo_r,
):
    r = lax.axis_index("row")
    c = lax.axis_index("col")
    y, zc = r // 4, lax.rem(r, 4)
    x, zl = c // 2, lax.rem(c, 2)
    child, group = r // 8, lax.rem(r, 8)

    load_upd = [
        pltpu.make_async_copy(upd_hbm.at[:, :, pl.ds(b * BLK, BLK)], upd.at[b], load_sem.at[b]) for b in range(8)
    ]
    load_col = pltpu.make_async_copy(front_hbm.at[:, pl.ds(0, BLK)], fcol, load_sem.at[8])
    for copy in load_upd:
        copy.start()
    load_col.start()

    def col_to(dx, dz):
        return lax.rem(x + dx, 4) * 2 + lax.rem(zl + dz, 2)

    def col_from(dx, dz):
        return lax.rem(x + 4 - dx, 4) * 2 + lax.rem(zl + dz, 2)

    def zc_at(d):
        return lax.rem(zc // 2 + d // 2, 2) * 2 + lax.rem(zc + d % 2, 2)

    def row_at(dy, dzc):
        return lax.rem(y + dy, 4) * 4 + zc_at(dzc)

    def send(src, dst, ssem, rsem, to):
        copy = pltpu.make_async_remote_copy(
            src_ref=src, dst_ref=dst, send_sem=ssem, recv_sem=rsem, device_id=to, device_id_type=MESH
        )
        copy.start()
        return copy

    def arrived(dst, sem):
        pltpu.make_async_copy(dst, dst, sem).wait()

    flip_r, flip_c = child * 8 + c, lax.rem(r, 8)
    off_diag = lax.rem(r, 8) != c
    barrier = pltpu.get_barrier_semaphore()
    for dx, dz in COL_STEPS:
        pl.semaphore_signal(barrier, inc=1, device_id=(r, col_to(dx, dz)), device_id_type=MESH)
    for dy in range(4):
        for d in range(4):
            if dy or d:
                pl.semaphore_signal(barrier, inc=1, device_id=(row_at(dy, d), c), device_id_type=MESH)

    @pl.when(off_diag)
    def _():
        pl.semaphore_signal(barrier, inc=1, device_id=(flip_r, flip_c), device_id_type=MESH)

    def find(first, count, modulus, residue):
        at = jnp.int32(0)
        for i in range(count):
            at = jnp.where(lax.rem(cm[child, first + i], modulus) == residue, i, at)
        return at

    block_row = [find(group * 8, 8, 8, (q % 2) * 4 + q // 2) for q in range(8)]

    for copy in load_upd:
        copy.wait()
    pl.semaphore_wait(barrier, 22 + off_diag.astype(jnp.int32))

    def pack(dst, at, to_col):
        block_col = find(c * 8, 8, 8, to_col)
        for q in range(8):
            dst[at, q] = upd[block_col, block_row[q]]

    sends = []
    for t, (dx, dz) in enumerate(COL_STEPS):
        to = col_to(dx, dz)
        pack(s1, to, to)
        sends.append(send(s1.at[to], r1.at[c], c_s.at[t], c_r.at[t], (r, to)))
    pack(r1, c, c)
    r1[8] = jnp.zeros((8, BLK, BLK), jnp.bfloat16)
    rw[16] = jnp.zeros((BLK, BLK), jnp.bfloat16)

    def col_table(at, carry):
        slot = jnp.int32(0)
        for i in range(8):
            entry = cm[at // 8, lax.rem(at, 8) * 8 + i]
            slot = jnp.where(lax.rem(entry, 8) == c, lax.div(entry, 8), slot)
        tab[16 + at] = slot
        return carry

    lax.fori_loop(0, 16, col_table, 0)

    def row_table(s):
        def step(e, found):
            entry = cm[s, e]
            return tuple(jnp.where(entry == l * 16 + r, s * 8 + e // 8, found[l]) for l in range(8))

        found = lax.fori_loop(0, 64, step, (jnp.int32(16),) * 8)
        for l in range(8):
            tab[s * 8 + l] = found[l]

    row_table(0)
    row_table(1)

    own_col = [c] + [col_from(dx, dz) for dx, dz in COL_STEPS]

    def z_stage(t):
        c0 = own_col[t]
        for d in range(1, 4):
            to = zc_at(d)
            sends.append(
                send(r1.at[c0, pl.ds(to * 2, 2)], r2.at[c0, :, zc], z_s.at[t, d - 1], z_r.at[t, d - 1], (y * 4 + to, c))
            )
        pltpu.make_async_copy(r1.at[c0, pl.ds(zc * 2, 2)], r2.at[c0, :, zc], z_l.at[t]).start()

    def y_stage(t):
        c0 = own_col[t]
        for d in range(1, 4):
            arrived(r2.at[c0, :, zc_at(d)], z_r.at[t, d - 1])
        arrived(r2.at[c0, :, zc], z_l.at[t])
        for dy in range(1, 4):
            to = lax.rem(y + dy, 4)
            sends.append(
                send(r2.at[c0, lax.rem(to, 2)], r3.at[y, c0], y_s.at[t, dy - 1], y_r.at[t, dy - 1], (to * 4 + zc, c))
            )
        pltpu.make_async_copy(r2.at[c0, lax.rem(y, 2)], r3.at[y, c0], y_l.at[t]).start()

    in_window = c < 4

    def window_send():
        source = jnp.int32(8)
        for i in range(8):
            source = jnp.where(tab[16 + child * 8 + i] == 0, i, source)
        for q in range(8):
            wsel[q] = r1[source, q]
        for dy in range(4):
            for d in range(4):
                i = dy * 4 + d
                to_y, to_zc = lax.rem(y + dy, 4), zc_at(d)
                src = wsel.at[to_zc * 2 + lax.rem(to_y, 2)]
                if i == 0:
                    pltpu.make_async_copy(src, rw.at[r], w_l).start()
                else:
                    send(src, rw.at[r], w_s.at[i], w_r.at[i], (to_y * 4 + to_zc, c))

    z_stage(0)
    for t in range(1, 8):
        arrived(r1.at[own_col[t]], c_r.at[t - 1])
        if t == 7:
            pl.when(in_window)(window_send)
        z_stage(t)
        y_stage(t - 1)
    y_stage(7)

    load_col.wait()

    @pl.when(in_window)
    def _():
        for dy in range(4):
            for d in range(4):
                i = dy * 4 + d
                src = lax.rem(y + 4 - dy, 4) * 4 + zc_at(d)
                arrived(rw.at[src], w_r.at[i] if i else w_l)
        for l in range(8):
            total = fcol[pl.ds(l * BLK, BLK), :]
            for s in range(2):
                total = total + rw[tab[s * 8 + l]].astype(jnp.float32)
            acol[l] = total
        ab[c] = acol[c]
        for l in range(8):
            @pl.when(c != l)
            def _():
                send(acol.at[l], ab.at[c], a_s.at[l], a_r.at[c], (r, l))

        @pl.when((r >= 1) & (r <= 3) & (c < r))
        def _():
            tp[c] = acol[0, pl.ds(pl.multiple_of(c * 16, 16), 16), :]
            for l in range(8):
                @pl.when(c != l)
                def _():
                    send(acol.at[0, pl.ds(l * 16, 16)], tp.at[c], tp_s.at[l], tp_r.at[c], (r, l))

    for i in (1, 2, 3):
        span = pl.ds(TOP_AT[i], i)

        @pl.when(r == i)
        def _():
            for k in range(i):
                @pl.when(c != k)
                def _():
                    arrived(tp.at[k], tp_r.at[k])
            tt[span] = tp[pl.ds(0, i)]
            for to in range(16):
                if to != i:
                    send(tp.at[pl.ds(0, i)], tt.at[span], tb_s.at[to], tb_r.at[i - 1], (to, c))

    for i in (1, 2, 3):
        span = pl.ds(TOP_AT[i], i)

        @pl.when(r != i)
        def _():
            arrived(tt.at[span], tb_r.at[i - 1])

    for t, (dx, dz) in enumerate(COL_STEPS):
        sends.append(send(tt, tf.at[c], tc_s.at[t], tc_r.at[t], (r, col_to(dx, dz))))
    tf[c] = tt[...]
    for t, (dx, dz) in enumerate(COL_STEPS):
        arrived(tf.at[col_from(dx, dz)], tc_r.at[t])
    for k in range(4):
        @pl.when(c != k)
        def _():
            arrived(ab.at[k], a_r.at[k])

    glob = c * 16 + r
    kept = []
    for k in range(4):
        parts = [ab[k]]
        for i in (1, 2, 3):
            if k < i:
                parts.append(tf[:, TOP_AT[i] + k].reshape(BLK, BLK))
        first = k + 1
        stack = jnp.concatenate(parts, axis=0) if len(parts) > 1 else parts[0]
        for j in range(k):
            rows_j, tops_j = kept[j]
            mine = [rows_j] + [tops_j[i] for i in range(first, 4)]
            mine = jnp.concatenate(mine, axis=0) if len(mine) > 1 else mine[0]
            stack = stack - lax.dot_general(
                mine, tops_j[k], (((1,), (1,)), ((), ())), preferred_element_type=jnp.float32
            )
        prod = lax.dot_general(
            stack, dinv[k], (((1,), (1,)), ((), ())), precision=HI, preferred_element_type=jnp.float32
        ).astype(jnp.bfloat16)
        own = prod[:BLK]
        own = jnp.where(glob > k, own, jnp.zeros_like(own))
        tops = {i: prod[(i - k) * BLK:(i - k + 1) * BLK] for i in range(first, 4)}
        kept.append((own, tops))
        lb[:, pl.ds(k * BLK, BLK)] = own

    @pl.when(off_diag)
    def _():
        send(lb, xa, al_s, al_r, (flip_r, flip_c))

    @pl.when(jnp.logical_not(off_diag))
    def _():
        pltpu.make_async_copy(lb, xa, al_r).start()

    for t, (dx, dz) in enumerate(COL_STEPS):
        sends.append(send(lb, lr.at[c], lr_s.at[t], lr_r.at[t], (r, col_to(dx, dz))))
    own_lr = pltpu.make_async_copy(lb, lr.at[c], lr_l)
    own_lr.start()

    arrived(xa, al_r)

    def slot(row):
        return 2 * lax.rem(row, 8) + row // 8

    spread = [(dy, d) for dy in range(4) for d in (0, 2) if dy or d]
    for i, (dy, d) in enumerate(spread):
        sends.append(send(xa, lc.at[slot(r)], be_s.at[i], be_r.at[i], (row_at(dy, d), c)))
    other = row_at(0, 1)
    sends.append(send(xa, lc.at[slot(r)], fo_s.at[7], fo_r.at[7], (other, c)))
    own_lc = pltpu.make_async_copy(xa, lc.at[slot(r)], be_l)
    own_lc.start()
    for i, (dy, d) in enumerate(spread):
        at = slot(lax.rem(y + 4 - dy, 4) * 4 + zc_at(d))
        arrived(lc.at[at], be_r.at[i])
        sends.append(send(lc.at[at], lc.at[at], fo_s.at[i], fo_r.at[i], (other, c)))

    for i, (dy, d) in enumerate(spread):
        arrived(lc.at[slot(lax.rem(y + 4 - dy, 4) * 4 + zc_at(d + 1))], fo_r.at[i])
    arrived(lc.at[slot(other)], fo_r.at[7])
    for t, (dx, dz) in enumerate(COL_STEPS):
        arrived(lr.at[col_from(dx, dz)], lr_r.at[t])
    own_lr.wait()
    own_lc.wait()
    for t in range(8):
        for dy in range(1, 4):
            arrived(r3.at[lax.rem(y + 4 - dy, 4), own_col[t]], y_r.at[t, dy - 1])
        arrived(r3.at[y, own_col[t]], y_l.at[t])
    for copy in sends:
        copy.wait_send()

    @pl.when(off_diag)
    def _():
        arrived(lb, al_s)

    @pl.when(in_window)
    def _():
        for i in range(1, 16):
            arrived(wsel.at[0], w_s.at[i])
        for l in range(8):
            @pl.when(c != l)
            def _():
                arrived(acol.at[l], a_s.at[l])

        @pl.when((r >= 1) & (r <= 3) & (c < r))
        def _():
            for l in range(8):
                @pl.when(c != l)
                def _():
                    arrived(acol.at[0, pl.ds(l * 16, 16)], tp_s.at[l])

    for i in (1, 2, 3):
        @pl.when(r == i)
        def _():
            for to in range(16):
                if to != i:
                    arrived(tp.at[pl.ds(0, i)], tb_s.at[to])


def exchange(child_map, child_upd, front, diag_inv):
    bf, f32 = jnp.bfloat16, jnp.float32
    dma = pltpu.SemaphoreType.DMA
    any_spec = pl.BlockSpec(memory_space=pl.ANY)
    smem = pl.BlockSpec(memory_space=pltpu.SMEM)
    return pl.pallas_call(
        exchange_kernel,
        out_shape=(
            jax.ShapeDtypeStruct((4, 8, 4, BLK, BLK), bf),
            jax.ShapeDtypeStruct((8, BLK, 4 * BLK), bf),
            jax.ShapeDtypeStruct((16, BLK, 4 * BLK), bf),
            jax.ShapeDtypeStruct((32,), jnp.int32),
        ),
        in_specs=[smem, any_spec, any_spec, pl.BlockSpec(memory_space=pltpu.VMEM)],
        out_specs=(any_spec, any_spec, any_spec, smem),
        scratch_shapes=[
            pltpu.VMEM((8, 8, BLK, BLK), bf),
            pltpu.VMEM((8 * BLK, BLK), f32),
            pltpu.VMEM((8, 8, BLK, BLK), bf),
            pltpu.VMEM((9, 8, BLK, BLK), bf),
            pltpu.VMEM((8, 2, 4, BLK, BLK), bf),
            pltpu.VMEM((8, BLK, BLK), bf),
            pltpu.VMEM((17, BLK, BLK), bf),
            pltpu.VMEM((8, BLK, BLK), f32),
            pltpu.VMEM((4, BLK, BLK), f32),
            pltpu.VMEM((4, 16, BLK), f32),
            pltpu.VMEM((6, 16, BLK), f32),
            pltpu.VMEM((8, 6, 16, BLK), f32),
            pltpu.VMEM((BLK, 4 * BLK), bf),
            pltpu.VMEM((BLK, 4 * BLK), bf),
            dma((9,)), dma((7,)), dma((7,)), dma((8, 3)), dma((8, 3)), dma((8,)),
            dma((8, 3)), dma((8, 3)), dma((8,)), dma((16,)), dma((16,)), dma,
            dma((8,)), dma((4,)), dma((8,)), dma((4,)), dma((16,)), dma((3,)), dma((7,)), dma((7,)),
            dma((7,)), dma((7,)), dma, dma, dma, dma((7,)), dma((7,)), dma, dma((8,)), dma((8,)),
        ],
        compiler_params=pltpu.CompilerParams(
            collective_id=0, has_side_effects=True, vmem_limit_bytes=60 * 2**20
        ),
    )(child_map, child_upd.reshape(8, BLK, 8 * BLK), front, diag_inv)


def update_kernel(tab, front, rows, cols, upd0, upd1, out, panels):
    l = pl.program_id(0)
    panels[...] = rows[0]
    out[...] = front[...] - lax.dot_general(
        rows[0], cols[...].reshape(16 * BLK, 4 * BLK), (((1,), (1,)), ((), ())),
        preferred_element_type=jnp.float32,
    )
    for s, upd in ((0, upd0), (1, upd1)):
        @pl.when(tab[s * 8 + l] < 16)
        def _():
            for c0 in range(8):
                at = pl.ds(pl.multiple_of(tab[16 + s * 8 + c0] * BLK, BLK), BLK)
                out[:, at] += upd[0, c0, 0].astype(jnp.float32)


def update(tab, front, rows, cols, arrived):
    def upd_spec(s):
        def index(l, tab):
            source = jnp.minimum(tab[s * 8 + l], 15)
            return (source // 4, 0, lax.rem(source, 4), 0, 0)

        return pl.BlockSpec((1, 8, 1, BLK, BLK), index)

    return pl.pallas_call(
        update_kernel,
        out_shape=(
            jax.ShapeDtypeStruct(front.shape, jnp.float32),
            jax.ShapeDtypeStruct((8 * BLK, 4 * BLK), jnp.bfloat16),
        ),
        grid_spec=pltpu.PrefetchScalarGridSpec(
            num_scalar_prefetch=1,
            grid=(8,),
            in_specs=[
                pl.BlockSpec((BLK, 16 * BLK), lambda l, tab: (l, 0)),
                pl.BlockSpec((1, BLK, 4 * BLK), lambda l, tab: (l, 0, 0)),
                pl.BlockSpec((16, BLK, 4 * BLK), lambda l, tab: (0, 0, 0)),
                upd_spec(0),
                upd_spec(1),
            ],
            out_specs=(
                pl.BlockSpec((BLK, 16 * BLK), lambda l, tab: (l, 0)),
                pl.BlockSpec((BLK, 4 * BLK), lambda l, tab: (l, 0)),
            ),
        ),
        compiler_params=pltpu.CompilerParams(vmem_limit_bytes=60 * 2**20),
    )(tab, front, rows, cols, arrived, arrived)


def on_device(front, child_upd, child_map, diag_inv):
    arrived, rows, cols, tab = exchange(child_map, child_upd, front, diag_inv)
    return update(tab, front, rows, cols, arrived)


def solution(mesh):
    return jax.shard_map(
        on_device,
        mesh=mesh,
        in_specs=(P("row", "col"), P("row", "col"), P(), P()),
        out_specs=(P("row", "col"), P("row", None)),
        check_vma=False,
    )


P = jax.sharding.PartitionSpec
```

time: 1040 us -> 153 us (0.15)
  the two profiles are of different devices: /device:TPU:1 before, /device:TPU:3 now
where the time goes in v1:
time: 153 us
  Pallas kernels  152 us (99%)
    pallas_call x1, Pallas kernels, exchange(): pl.pallas_call(exchange_kernel, out_shape=(jax.ShapeDtypeStruct((4, 8, 4,...  138 us
    pallas_call x1, Pallas kernels, update(): pl.pallas_call(update_kernel, out_shape=(jax.ShapeDtypeStruct(front.shape...  14 us

profile of v1, /device:TPU:3, one launch (start us, length us, event | category | flops | bytes accessed | tf_op | source)
XLA Modules:
  0.0 152.5 jit_solution(5142172658723448410)
XLA Ops:
  0.6 137.9 %shard_map.59 = (bf16[4,8,4,128,128]{4,3,2,1,0:T(8,128)(2,1)}, bf16[8,128,512]{2,1,0:T(8,128)(2,1)}, bf16[16,128,512]{2,1,0:T(8,128)(2,1)}, s32[32]{0:T(128)}) custom-call(s32[2,64]{1,0:T(2,128)} %cm.1, bf16[8,128,1024]{2,1,0:T(8,128)(2,1)} %bitcast.1, f32[1024,2048]{1,0:T(8,128)} %front.1, f32[4,128,128]{2,1,0:T(8,128)} %dinv.1), custom_call_target="tpu_custom_call" | custom-call | tf_op jit(solution)/shard_map/pallas_call | solution.py:331
  138.5 14.0 %shard_map.60 = (f32[1024,2048]{1,0:T(8,128)}, bf16[1024,512]{1,0:T(8,128)(2,1)}) custom-call(s32[32]{0:T(128)} %get-tuple-element.6.tab, f32[1024,2048]{1,0:T(8,128)} %front.1, bf16[8,128,512]{2,1,0:T(8,128)(2,1)} %get-tuple-element.7.rows, bf16[16,128,512]{2,1,0:T(8,128)(2,1)} %get-tuple-element.8.cols, ...), custom_call_target="tpu_custom_call" | custom-call | tf_op jit(solution)/shard_map/pallas_call | solution.py:390

commit v2 on v1

v2 whole, which is shorter than its diff:
```python
import jax
import jax.numpy as jnp
from jax import lax
from jax.experimental import pallas as pl
from jax.experimental.pallas import tpu as pltpu

MESH = pl.DeviceIdType.MESH
BLK = 128
HI = lax.Precision.HIGHEST
COL_STEPS = ((0, 1), (1, 0), (3, 0), (1, 1), (3, 1), (2, 0), (2, 1))
TOP_AT = (0, 0, 1, 3)


def exchange_kernel(
    cm, upd_hbm, front_hbm, dinv_hbm,
    r3, lr, lc, fvm, tab,
    upd, fcol, dinv, s1, r1, r2, wsel, rw, acol, ab, tops, tpart, tsum, tall, tp, tt, tmix, tf, bt, lb, xa, lp,
    load_sem, c_s, c_r, z_s, z_r, z_l, y_s, y_r, y_l, w_s, w_r, w_l,
    a_s, a_r, te_s, te_r, tv_s, tv_r, tp_s, tp_r, tb_s, tb_r, tc_s, tc_r,
    lp_s, lp_r, lr_s, lr_r, lr_l, al_s, al_r, be_s, be_r, be_l, fo_s, fo_r,
):
    r = lax.axis_index("row")
    c = lax.axis_index("col")
    y, zc = r // 4, lax.rem(r, 4)
    x, zl = c // 2, lax.rem(c, 2)
    child, group = r // 8, lax.rem(r, 8)

    load_upd = [
        pltpu.make_async_copy(upd_hbm.at[:, :, pl.ds(b * BLK, BLK)], upd.at[b], load_sem.at[b]) for b in range(8)
    ]
    load_col = pltpu.make_async_copy(front_hbm.at[:, pl.ds(0, BLK)], fcol, load_sem.at[8])
    for copy in load_upd:
        copy.start()
    load_col.start()
    load_dinv = pltpu.make_async_copy(dinv_hbm, dinv, load_sem.at[10])
    load_dinv.start()
    load_front = pltpu.make_async_copy(front_hbm, fvm, load_sem.at[9])

    def col_to(dx, dz):
        return lax.rem(x + dx, 4) * 2 + lax.rem(zl + dz, 2)

    def col_from(dx, dz):
        return lax.rem(x + 4 - dx, 4) * 2 + lax.rem(zl + dz, 2)

    def zc_at(d):
        return lax.rem(zc // 2 + d // 2, 2) * 2 + lax.rem(zc + d % 2, 2)

    def row_at(dy, dzc):
        return lax.rem(y + dy, 4) * 4 + zc_at(dzc)

    def send(src, dst, ssem, rsem, to):
        copy = pltpu.make_async_remote_copy(
            src_ref=src, dst_ref=dst, send_sem=ssem, recv_sem=rsem, device_id=to, device_id_type=MESH
        )
        copy.start()
        return copy

    def arrived(dst, sem):
        pltpu.make_async_copy(dst, dst, sem).wait()

    flip_r, flip_c = child * 8 + c, lax.rem(r, 8)
    flip_r2 = child * 8 + lax.rem(c // 2 + 1, 2) * 2 + c // 4 * 4 + lax.rem(c, 2)
    flip_c2 = lax.rem(flip_c // 2 + 1, 2) * 2 + flip_c // 4 * 4 + lax.rem(flip_c, 2)
    off_diag = lax.rem(r, 8) != c
    pair_at = lax.rem(c // 2, 2)
    barrier = pltpu.get_barrier_semaphore()
    for dx, dz in COL_STEPS:
        pl.semaphore_signal(barrier, inc=1, device_id=(r, col_to(dx, dz)), device_id_type=MESH)
    for dy in range(4):
        for d in range(4):
            if dy or d:
                pl.semaphore_signal(barrier, inc=1, device_id=(row_at(dy, d), c), device_id_type=MESH)

    @pl.when(off_diag)
    def _():
        pl.semaphore_signal(barrier, inc=1, device_id=(flip_r, flip_c), device_id_type=MESH)

    pl.semaphore_signal(barrier, inc=1, device_id=(flip_r, flip_c2), device_id_type=MESH)

    def residues(first):
        return [cm[child, first + i] & 7 for i in range(8)]

    def find(values, wanted):
        at = jnp.int32(0)
        for i in range(1, 8):
            at = jnp.where(values[i] == wanted, i, at)
        return at

    row_residues, col_residues = residues(group * 8), residues(c * 8)
    block_row = [find(row_residues, (q % 2) * 4 + q // 2) for q in range(8)]

    for copy in load_upd:
        copy.wait()

    def pack(dst, at, to_col):
        block_col = find(col_residues, to_col)
        for q in range(8):
            dst[at, q] = upd[block_col, block_row[q]]

    sends = []

    def c_send(t):
        to = col_to(*COL_STEPS[t])
        sends.append(send(s1.at[to], r1.at[c], c_s.at[t], c_r.at[t], (r, to)))

    def sixteen(at):
        return pl.ds(pl.multiple_of(at * 16, 16), 16)

    for dx, dz in COL_STEPS:
        to = col_to(dx, dz)
        pack(s1, to, to)
    pl.semaphore_wait(barrier, 23 + off_diag.astype(jnp.int32))
    for t in range(3):
        c_send(t)
    pack(r1, c, c)
    r1[8] = jnp.zeros((8, BLK, BLK), jnp.bfloat16)
    rw[16] = jnp.zeros((BLK, BLK), jnp.bfloat16)
    upd[8] = jnp.zeros((8, BLK, BLK), jnp.bfloat16)

    def col_table(at, carry):
        slot = jnp.int32(0)
        for i in range(8):
            entry = cm[at >> 3, (at & 7) * 8 + i]
            slot = jnp.where((entry & 7) == c, entry >> 3, slot)
        tab[16 + at] = slot
        return carry

    lax.fori_loop(0, 16, col_table, 0)

    def row_table(s):
        def step(e, found):
            entry = cm[s, e]
            here = s * 8 + (e >> 3)
            return tuple(jnp.where(entry == l * 16 + r, here, found[l]) for l in range(8))

        found = lax.fori_loop(0, 64, step, (jnp.int32(16),) * 8)
        for l in range(8):
            tab[s * 8 + l] = found[l]

    row_table(0)
    row_table(1)

    own_col = [c] + [col_from(dx, dz) for dx, dz in COL_STEPS]

    def c_wait(t):
        arrived(r1.at[own_col[t]], c_r.at[t - 1])

    def z_stage(t):
        c0 = own_col[t]
        for d in range(1, 4):
            to = zc_at(d)
            sends.append(
                send(r1.at[c0, pl.ds(to * 2, 2)], r2.at[c0, :, zc], z_s.at[t, d - 1], z_r.at[t, d - 1], (y * 4 + to, c))
            )
        pltpu.make_async_copy(r1.at[c0, pl.ds(zc * 2, 2)], r2.at[c0, :, zc], z_l.at[t]).start()

    def y_stage(t):
        c0 = own_col[t]
        for d in range(1, 4):
            arrived(r2.at[c0, :, zc_at(d)], z_r.at[t, d - 1])
        arrived(r2.at[c0, :, zc], z_l.at[t])
        for dy in range(1, 4):
            to = lax.rem(y + dy, 4)
            sends.append(
                send(r2.at[c0, lax.rem(to, 2)], r3.at[y, c0], y_s.at[t, dy - 1], y_r.at[t, dy - 1], (to * 4 + zc, c))
            )
        pltpu.make_async_copy(r2.at[c0, lax.rem(y, 2)], r3.at[y, c0], y_l.at[t]).start()

    in_window = c < 4

    def window_send():
        source = jnp.int32(8)
        for i in range(8):
            source = jnp.where(tab[16 + child * 8 + i] == 0, i, source)
        for q in range(8):
            wsel[q] = r1[source, q]
        for dy in range(4):
            for d in range(4):
                i = dy * 4 + d
                to_y, to_zc = lax.rem(y + dy, 4), zc_at(d)
                src = wsel.at[to_zc * 2 + lax.rem(to_y, 2)]
                if i == 0:
                    pltpu.make_async_copy(src, rw.at[r], w_l).start()
                else:
                    send(src, rw.at[r], w_s.at[i], w_r.at[i], (to_y * 4 + to_zc, c))

    pumped = {}

    def pump(t):
        if t - 3 in pumped:
            for copy in pumped.pop(t - 3):
                copy.wait_send()
        first = len(sends)
        y_stage(t)
        pumped[t] = sends[first:]
        del sends[first:]

    def find_equal(first, value, none):
        at = jnp.int32(none)
        for i in range(8):
            at = jnp.where(cm[child, first + i] == value, i, at)
        return at

    z_stage(0)
    top_row = [find_equal(group * 8, i, 8) for i in (1, 2, 3)]
    top_col = [find_equal(c * 8, k, 8) for k in range(3)]
    for i in (1, 2, 3):
        for k in range(i):
            at_col = jnp.where(top_row[i - 1] == 8, 8, top_col[k])
            tops[TOP_AT[i] + k] = upd[at_col, jnp.minimum(top_row[i - 1], 7)]
    for t, (dx, dz) in enumerate(COL_STEPS):
        to = col_to(dx, dz)
        sends.append(send(tops.at[:, sixteen(to)], tpart.at[c], te_s.at[t], te_r.at[t], (r, to)))
    tpart[c] = tops[:, sixteen(c), :]
    for t in range(3, 6):
        c_send(t)
    load_col.wait()
    load_dinv.wait()
    holds_top = (r >= 1) & (r <= 3) & (c < r)

    @pl.when(holds_top)
    def _():
        tp[c] = fcol[sixteen(c), :]
        for l in range(8):
            @pl.when(c != l)
            def _():
                send(fcol.at[pl.ds(l * 16, 16)], tp.at[c], tp_s.at[l], tp_r.at[c], (r, l))

    load_front.start()
    pump(0)
    for t in (1, 2, 3):
        c_wait(t)
        z_stage(t)
    c_send(6)

    for t, (dx, dz) in enumerate(COL_STEPS):
        arrived(tpart.at[col_from(dx, dz)], te_r.at[t])
    total = tpart[0].astype(jnp.float32)
    for i in range(1, 8):
        total = total + tpart[i].astype(jnp.float32)
    tsum[...] = total.astype(jnp.bfloat16)
    for dy in range(4):
        for d in range(4):
            i = dy * 4 + d
            if i:
                sends.append(send(tsum, tall.at[r], tv_s.at[i], tv_r.at[i], (row_at(dy, d), c)))
    tall[r] = tsum[...]
    for i in (1, 2, 3):
        span = pl.ds(TOP_AT[i], i)

        @pl.when(r == i)
        def _():
            for k in range(i):
                @pl.when(c != k)
                def _():
                    arrived(tp.at[k], tp_r.at[k])
            tt[span] = tp[pl.ds(0, i)]
            for to in range(16):
                if to != i:
                    send(tp.at[pl.ds(0, i)], tt.at[span], tb_s.at[to], tb_r.at[i - 1], (to, c))

    pump(1)
    for t in (4, 5, 6):
        c_wait(t)
        z_stage(t)
    pump(2)
    pump(3)

    for i in (1, 2, 3):
        span = pl.ds(TOP_AT[i], i)

        @pl.when(r != i)
        def _():
            arrived(tt.at[span], tb_r.at[i - 1])

    for dy in range(4):
        for d in range(4):
            i = dy * 4 + d
            if i:
                arrived(tall.at[lax.rem(y + 4 - dy, 4) * 4 + zc_at(d)], tv_r.at[i])
    total = tt[...]
    for i in range(16):
        total = total + tall[i].astype(jnp.float32)
    tmix[...] = total
    for t, (dx, dz) in enumerate(COL_STEPS):
        sends.append(send(tmix, tf.at[c], tc_s.at[t], tc_r.at[t], (r, col_to(dx, dz))))
    tf[c] = tmix[...]

    c_wait(7)
    pl.when(in_window)(window_send)
    z_stage(7)
    pump(4)

    for t, (dx, dz) in enumerate(COL_STEPS):
        arrived(tf.at[col_from(dx, dz)], tc_r.at[t])

    def outer(a, b):
        return lax.dot_general(a, b, (((1,), (1,)), ((), ())), preferred_element_type=jnp.float32)

    def solve(a, k):
        return lax.dot_general(
            a, dinv[k], (((1,), (1,)), ((), ())), precision=HI, preferred_element_type=jnp.float32
        ).astype(jnp.bfloat16)

    for k in range(3):
        stack = []
        for i in range(k + 1, 4):
            block = tf[:, TOP_AT[i] + k].reshape(BLK, BLK)
            for j in range(k):
                block = block - outer(bt[TOP_AT[i] + j], bt[TOP_AT[k] + j])
            stack.append(block)
        prod = solve(jnp.concatenate(stack, axis=0), k)
        for i in range(k + 1, 4):
            bt[TOP_AT[i] + k] = prod[(i - k - 1) * BLK:(i - k) * BLK]

    pump(5)

    @pl.when(in_window)
    def _():
        for dy in range(4):
            for d in range(4):
                i = dy * 4 + d
                src = lax.rem(y + 4 - dy, 4) * 4 + zc_at(d)
                arrived(rw.at[src], w_r.at[i] if i else w_l)
        for l in range(8):
            total = fcol[pl.ds(l * BLK, BLK), :]
            for s in range(2):
                total = total + rw[tab[s * 8 + l]].astype(jnp.float32)
            acol[l] = total
        ab[c] = acol[c]
        for l in range(8):
            @pl.when(c != l)
            def _():
                send(acol.at[l], ab.at[c], a_s.at[l], a_r.at[c], (r, l))

    pump(6)
    for k in range(4):
        @pl.when(c != k)
        def _():
            arrived(ab.at[k], a_r.at[k])

    glob = c * 16 + r
    kept = []
    for k in range(4):
        block = ab[k]
        for j in range(k):
            block = block - outer(kept[j], bt[TOP_AT[k] + j])
        panel = solve(block, k)
        panel = jnp.where(glob > k, panel, jnp.zeros_like(panel))
        kept.append(panel)
        lb[:, pl.ds(k * BLK, BLK)] = panel

    zh, core = zc // 2, lax.rem(zc, 2)
    sends.append(send(lb, xa.at[pair_at], al_s.at[1], al_r.at[1], (flip_r2, flip_c)))

    @pl.when(off_diag)
    def _():
        send(lb, xa.at[pair_at], al_s.at[0], al_r.at[0], (flip_r, flip_c))

    @pl.when(jnp.logical_not(off_diag))
    def _():
        pltpu.make_async_copy(lb, xa.at[pair_at], al_r.at[0]).start()

    sends.append(send(lb, lp.at[zl], lp_s, lp_r, (r, col_to(0, 1))))
    lp[zl] = lb[...]

    def x_at(dx):
        return lax.rem(x + dx, 4)

    arrived(lp.at[lax.rem(zl + 1, 2)], lp_r)
    for dx in (1, 3, 2):
        sends.append(send(lp, lr.at[x], lr_s.at[dx], lr_r.at[dx], (r, x_at(dx) * 2 + zl)))
    own_lr = pltpu.make_async_copy(lp, lr.at[x], lr_l)
    own_lr.start()

    pump(7)
    arrived(xa.at[zh], al_r.at[0])
    arrived(xa.at[lax.rem(zh + 1, 2)], al_r.at[1])
    other = row_at(0, 1)
    for dy in (1, 3, 2):
        sends.append(send(xa, lc.at[y, core], be_s.at[dy], be_r.at[dy], (row_at(dy, 0), c)))
    sends.append(send(xa, lc.at[y, core], fo_s.at[0], fo_r.at[0], (other, c)))
    own_lc = pltpu.make_async_copy(xa, lc.at[y, core], be_l)
    own_lc.start()
    for dy in (1, 3, 2):
        at = lc.at[lax.rem(y + 4 - dy, 4), core]
        arrived(at, be_r.at[dy])
        sends.append(send(at, at, fo_s.at[dy], fo_r.at[dy], (other, c)))

    load_front.wait()
    for dy in range(4):
        arrived(lc.at[lax.rem(y + 4 - dy, 4), lax.rem(core + 1, 2)], fo_r.at[dy])
    for dx in (1, 3, 2):
        arrived(lr.at[x_at(4 - dx)], lr_r.at[dx])
    own_lr.wait()
    own_lc.wait()
    for t in range(8):
        for dy in range(1, 4):
            arrived(r3.at[lax.rem(y + 4 - dy, 4), own_col[t]], y_r.at[t, dy - 1])
        arrived(r3.at[y, own_col[t]], y_l.at[t])
    for copies in [sends, *pumped.values()]:
        for copy in copies:
            copy.wait_send()

    @pl.when(off_diag)
    def _():
        arrived(lb, al_s.at[0])

    @pl.when(in_window)
    def _():
        for i in range(1, 16):
            arrived(wsel.at[0], w_s.at[i])
        for l in range(8):
            @pl.when(c != l)
            def _():
                arrived(acol.at[l], a_s.at[l])

    @pl.when(holds_top)
    def _():
        for l in range(8):
            @pl.when(c != l)
            def _():
                arrived(fcol.at[pl.ds(l * 16, 16)], tp_s.at[l])

    for i in (1, 2, 3):
        @pl.when(r == i)
        def _():
            for to in range(16):
                if to != i:
                    arrived(tp.at[pl.ds(0, i)], tb_s.at[to])


def exchange(child_map, child_upd, front, diag_inv):
    bf, f32 = jnp.bfloat16, jnp.float32
    dma = pltpu.SemaphoreType.DMA
    any_spec = pl.BlockSpec(memory_space=pl.ANY)
    smem = pl.BlockSpec(memory_space=pltpu.SMEM)
    return pl.pallas_call(
        exchange_kernel,
        out_shape=(
            pltpu.VMEM((4, 8, 4, BLK, BLK), bf),
            pltpu.VMEM((4, 2, BLK, 4 * BLK), bf),
            pltpu.VMEM((4, 2, 2, BLK, 4 * BLK), bf),
            pltpu.VMEM(front.shape, f32),
            jax.ShapeDtypeStruct((32,), jnp.int32),
        ),
        in_specs=[smem, any_spec, any_spec, any_spec],
        out_specs=(any_spec, any_spec, any_spec, any_spec, smem),
        scratch_shapes=[
            pltpu.VMEM((9, 8, BLK, BLK), bf),
            pltpu.VMEM((8 * BLK, BLK), f32),
            pltpu.VMEM((4, BLK, BLK), f32),
            pltpu.VMEM((8, 8, BLK, BLK), bf),
            pltpu.VMEM((9, 8, BLK, BLK), bf),
            pltpu.VMEM((8, 2, 4, BLK, BLK), bf),
            pltpu.VMEM((8, BLK, BLK), bf),
            pltpu.VMEM((17, BLK, BLK), bf),
            pltpu.VMEM((8, BLK, BLK), f32),
            pltpu.VMEM((4, BLK, BLK), f32),
            pltpu.VMEM((6, BLK, BLK), bf),
            pltpu.VMEM((8, 6, 16, BLK), bf),
            pltpu.VMEM((6, 16, BLK), bf),
            pltpu.VMEM((16, 6, 16, BLK), bf),
            pltpu.VMEM((4, 16, BLK), f32),
            pltpu.VMEM((6, 16, BLK), f32),
            pltpu.VMEM((6, 16, BLK), f32),
            pltpu.VMEM((8, 6, 16, BLK), f32),
            pltpu.VMEM((6, BLK, BLK), bf),
            pltpu.VMEM((BLK, 4 * BLK), bf),
            pltpu.VMEM((2, BLK, 4 * BLK), bf),
            pltpu.VMEM((2, BLK, 4 * BLK), bf),
            dma((11,)), dma((7,)), dma((7,)), dma((8, 3)), dma((8, 3)), dma((8,)),
            dma((8, 3)), dma((8, 3)), dma((8,)), dma((16,)), dma((16,)), dma,
            dma((8,)), dma((4,)), dma((7,)), dma((7,)), dma((16,)), dma((16,)),
            dma((8,)), dma((4,)), dma((16,)), dma((3,)), dma((7,)), dma((7,)),
            dma, dma, dma((4,)), dma((4,)), dma, dma((2,)), dma((2,)), dma((4,)), dma((4,)), dma, dma((4,)), dma((4,)),
        ],
        compiler_params=pltpu.CompilerParams(
            collective_id=0, has_side_effects=True, vmem_limit_bytes=48 * 2**20
        ),
    )(child_map, child_upd.reshape(8, BLK, 8 * BLK), front, diag_inv)


def update_kernel(tab, front, rows, cols, arrived, out, panels, stage, out_sem, panel_sem):
    copy_panels = pltpu.make_async_copy(rows, panels, panel_sem)
    copy_panels.start()
    mine = rows[...].reshape(8 * BLK, 4 * BLK)
    copies = []
    for t in range(8):
        at = pl.ds(t * 2 * BLK, 2 * BLK)
        pair = jnp.concatenate([cols[t // 4, t % 2, t // 2 % 2], cols[2 + t // 4, t % 2, t // 2 % 2]], axis=0)
        if t >= 2:
            copies[t - 2].wait()
        stage[t % 2] = front[:, at] - lax.dot_general(
            mine, pair, (((1,), (1,)), ((), ())), preferred_element_type=jnp.float32
        )
        for s in range(2):
            for j in range(2):
                c0 = source_col(tab, s, 2 * t + j)

                @pl.when(c0 >= 0)
                def _():
                    @pl.loop(0, 8)
                    def _(l):
                        source = tab[s * 8 + l]

                        @pl.when(source < 16)
                        def _():
                            here = (t % 2, pl.ds(pl.multiple_of(l * BLK, BLK), BLK), pl.ds(j * BLK, BLK))
                            stage[here] += arrived[source // 4, c0, lax.rem(source, 4)].astype(jnp.float32)
        copy = pltpu.make_async_copy(stage.at[t % 2], out.at[:, at], out_sem.at[t % 2])
        copy.start()
        copies.append(copy)
    copies[6].wait()
    copies[7].wait()
    copy_panels.wait()


def source_col(tab, s, slot):
    at = jnp.int32(-1)
    for i in range(8):
        at = jnp.where(tab[16 + s * 8 + i] == slot, i, at)
    return at


def update(tab, front, rows, cols, arrived):
    vmem = pl.BlockSpec(memory_space=pltpu.VMEM)
    any_spec = pl.BlockSpec(memory_space=pl.ANY)
    out, panels = pl.pallas_call(
        update_kernel,
        out_shape=(
            jax.ShapeDtypeStruct(front.shape, jnp.float32),
            jax.ShapeDtypeStruct((8, BLK, 4 * BLK), jnp.bfloat16),
        ),
        in_specs=[pl.BlockSpec(memory_space=pltpu.SMEM), vmem, vmem, vmem, vmem],
        out_specs=(any_spec, any_spec),
        scratch_shapes=[
            pltpu.VMEM((2, 8 * BLK, 2 * BLK), jnp.float32),
            pltpu.SemaphoreType.DMA((2,)),
            pltpu.SemaphoreType.DMA,
        ],
        compiler_params=pltpu.CompilerParams(vmem_limit_bytes=24 * 2**20),
    )(tab, front, rows.reshape(8, BLK, 4 * BLK), cols, arrived)
    return out, panels.reshape(8 * BLK, 4 * BLK)


def on_device(front, child_upd, child_map, diag_inv):
    arrived, rows, cols, front_near, tab = exchange(child_map, child_upd, front, diag_inv)
    return update(tab, front_near, rows, cols, arrived)


def solution(mesh):
    return jax.shard_map(
        on_device,
        mesh=mesh,
        in_specs=(P("row", "col"), P("row", "col"), P(), P()),
        out_specs=(P("row", "col"), P("row", None)),
        check_vma=False,
    )


P = jax.sharding.PartitionSpec
```

time: 153 us -> 131 us (0.86)
  the two profiles are of different devices: /device:TPU:3 before, /device:TPU:1 now
where the time goes in v2:
time: 131 us
  Pallas kernels  130 us (99%)
    pallas_call x1, Pallas kernels, exchange(): pl.pallas_call(exchange_kernel, out_shape=(pltpu.VMEM((4, 8, 4, BLK, BLK)...  120 us
    pallas_call x1, Pallas kernels, update(): pl.pallas_call(update_kernel, out_shape=(jax.ShapeDtypeStruct(front.shape...  10.2 us

profile of v2, /device:TPU:1, one launch (start us, length us, event | category | flops | bytes accessed | tf_op | source)
XLA Modules:
  0.0 131.2 jit_solution(15881348555297428049)
XLA Ops:
  0.6 119.6 %shard_map.59 = (bf16[4,8,4,128,128]{4,3,2,1,0:T(8,128)(2,1)S(1)}, bf16[4,2,128,512]{3,2,1,0:T(8,128)(2,1)S(1)}, bf16[4,2,2,128,512]{4,3,2,1,0:T(8,128)(2,1)S(1)}, f32[1024,2048]{1,0:T(8,128)S(1)}, s32[32]{0:T(128)}) custom-call(s32[2,64]{1,0:T(2,128)} %cm.1, bf16[8,128,1024]{2,1,0:T(8,128)(2,1)} %bitcast.4, f32[1024,2048]{1,0:T(8,128)} %front_hbm.1, ...), custom_call_target="tpu_custom_call" | custom-call | tf_op jit(solution)/shard_map/pallas_call | solution.py:438
  120.3 0.0 copy-start
  120.3 0.7 copy-done
  121.0 10.2 %shard_map.60 = (f32[1024,2048]{1,0:T(8,128)}, bf16[8,128,512]{2,1,0:T(8,128)(2,1)}) custom-call(s32[32]{0:T(128)S(1)} %copy-done, f32[1024,2048]{1,0:T(8,128)S(1)} %get-tuple-element.10.front, bf16[8,128,512]{2,1,0:T(8,128)(2,1)S(1)} %bitcast.3, bf16[4,2,2,128,512]{4,3,2,1,0:T(8,128)(2,1)S(1)} %get-tuple-element.12.cols, ...), custom_call_target="tpu_custom_call" | custom-call | tf_op jit(solution)/shard_map/pallas_call | solution.py:529
Async XLA Ops:
  120.3 0.7 copy-start

commit v3 on v2

--- a/solution.py
+++ b/solution.py
@@ -59,8 +59,6 @@
         pltpu.make_async_copy(dst, dst, sem).wait()
 
     flip_r, flip_c = child * 8 + c, lax.rem(r, 8)
-    flip_r2 = child * 8 + lax.rem(c // 2 + 1, 2) * 2 + c // 4 * 4 + lax.rem(c, 2)
-    flip_c2 = lax.rem(flip_c // 2 + 1, 2) * 2 + flip_c // 4 * 4 + lax.rem(flip_c, 2)
     off_diag = lax.rem(r, 8) != c
     pair_at = lax.rem(c // 2, 2)
     barrier = pltpu.get_barrier_semaphore()
@@ -75,8 +73,6 @@
     def _():
         pl.semaphore_signal(barrier, inc=1, device_id=(flip_r, flip_c), device_id_type=MESH)
 
-    pl.semaphore_signal(barrier, inc=1, device_id=(flip_r, flip_c2), device_id_type=MESH)
-
     def residues(first):
         return [cm[child, first + i] & 7 for i in range(8)]
 
@@ -109,7 +105,7 @@
     for dx, dz in COL_STEPS:
         to = col_to(dx, dz)
         pack(s1, to, to)
-    pl.semaphore_wait(barrier, 23 + off_diag.astype(jnp.int32))
+    pl.semaphore_wait(barrier, 22 + off_diag.astype(jnp.int32))
     for t in range(3):
         c_send(t)
     pack(r1, c, c)
@@ -351,7 +347,6 @@
         lb[:, pl.ds(k * BLK, BLK)] = panel
 
     zh, core = zc // 2, lax.rem(zc, 2)
-    sends.append(send(lb, xa.at[pair_at], al_s.at[1], al_r.at[1], (flip_r2, flip_c)))
 
     @pl.when(off_diag)
     def _():
@@ -374,22 +369,34 @@
     own_lr.start()
 
     pump(7)
+    other = row_at(0, 1)
+
+    def spread(at, i):
+        for dy in (1, 3, 2):
+            sends.append(send(xa.at[at], lc.at[y, core, at], be_s.at[i, dy], be_r.at[i, dy], (row_at(dy, 0), c)))
+        sends.append(send(xa.at[at], lc.at[y, core, at], fo_s.at[i, 0], fo_r.at[i, 0], (other, c)))
+
+    def forward(at, i):
+        for dy in (1, 3, 2):
+            here = lc.at[lax.rem(y + 4 - dy, 4), core, at]
+            arrived(here, be_r.at[i, dy])
+            sends.append(send(here, here, fo_s.at[i, dy], fo_r.at[i, dy], (other, c)))
+
+    far = 1 - zh
     arrived(xa.at[zh], al_r.at[0])
-    arrived(xa.at[lax.rem(zh + 1, 2)], al_r.at[1])
-    other = row_at(0, 1)
-    for dy in (1, 3, 2):
-        sends.append(send(xa, lc.at[y, core], be_s.at[dy], be_r.at[dy], (row_at(dy, 0), c)))
-    sends.append(send(xa, lc.at[y, core], fo_s.at[0], fo_r.at[0], (other, c)))
+    sends.append(send(xa.at[zh], xa.at[zh], al_s.at[1], al_r.at[1], (row_at(0, 2), c)))
+    spread(zh, 0)
+    arrived(xa.at[far], al_r.at[1])
+    spread(far, 1)
     own_lc = pltpu.make_async_copy(xa, lc.at[y, core], be_l)
     own_lc.start()
-    for dy in (1, 3, 2):
-        at = lc.at[lax.rem(y + 4 - dy, 4), core]
-        arrived(at, be_r.at[dy])
-        sends.append(send(at, at, fo_s.at[dy], fo_r.at[dy], (other, c)))
+    forward(zh, 0)
+    forward(far, 1)
 
     load_front.wait()
-    for dy in range(4):
-        arrived(lc.at[lax.rem(y + 4 - dy, 4), lax.rem(core + 1, 2)], fo_r.at[dy])
+    for i, at in ((0, zh), (1, far)):
+        for dy in range(4):
+            arrived(lc.at[lax.rem(y + 4 - dy, 4), 1 - core, at], fo_r.at[i, dy])
     for dx in (1, 3, 2):
         arrived(lr.at[x_at(4 - dx)], lr_r.at[dx])
     own_lr.wait()
@@ -473,7 +480,7 @@
             dma((8, 3)), dma((8, 3)), dma((8,)), dma((16,)), dma((16,)), dma,
             dma((8,)), dma((4,)), dma((7,)), dma((7,)), dma((16,)), dma((16,)),
             dma((8,)), dma((4,)), dma((16,)), dma((3,)), dma((7,)), dma((7,)),
-            dma, dma, dma((4,)), dma((4,)), dma, dma((2,)), dma((2,)), dma((4,)), dma((4,)), dma, dma((4,)), dma((4,)),
+            dma, dma, dma((4,)), dma((4,)), dma, dma((2,)), dma((2,)), dma((2, 4)), dma((2, 4)), dma, dma((2, 4)), dma((2, 4)),
         ],
         compiler_params=pltpu.CompilerParams(
             collective_id=0, has_side_effects=True, vmem_limit_bytes=48 * 2**20
@@ -484,29 +491,30 @@
 def update_kernel(tab, front, rows, cols, arrived, out, panels, stage, out_sem, panel_sem):
     copy_panels = pltpu.make_async_copy(rows, panels, panel_sem)
     copy_panels.start()
-    mine = rows[...].reshape(8 * BLK, 4 * BLK)
     copies = []
     for t in range(8):
         at = pl.ds(t * 2 * BLK, 2 * BLK)
         pair = jnp.concatenate([cols[t // 4, t % 2, t // 2 % 2], cols[2 + t // 4, t % 2, t // 2 % 2]], axis=0)
         if t >= 2:
             copies[t - 2].wait()
-        stage[t % 2] = front[:, at] - lax.dot_general(
-            mine, pair, (((1,), (1,)), ((), ())), preferred_element_type=jnp.float32
-        )
+        for part in range(2):
+            here = pl.ds(part * 4 * BLK, 4 * BLK)
+            mine = rows[pl.ds(part * 4, 4)].reshape(4 * BLK, 4 * BLK)
+            stage[t % 2, here, :] = front[here, at] - lax.dot_general(
+                mine, pair, (((1,), (1,)), ((), ())), preferred_element_type=jnp.float32
+            )
         for s in range(2):
             for j in range(2):
                 c0 = source_col(tab, s, 2 * t + j)
 
                 @pl.when(c0 >= 0)
                 def _():
-                    @pl.loop(0, 8)
-                    def _(l):
+                    for l in range(8):
                         source = tab[s * 8 + l]
 
                         @pl.when(source < 16)
                         def _():
-                            here = (t % 2, pl.ds(pl.multiple_of(l * BLK, BLK), BLK), pl.ds(j * BLK, BLK))
+                            here = (t % 2, pl.ds(l * BLK, BLK), pl.ds(j * BLK, BLK))
                             stage[here] += arrived[source // 4, c0, lax.rem(source, 4)].astype(jnp.float32)
         copy = pltpu.make_async_copy(stage.at[t % 2], out.at[:, at], out_sem.at[t % 2])
         copy.start()

time: 131 us -> 124 us (0.947)
  Pallas kernels: 130 us -> 123 us
    pallas_call x1, Pallas kernels: 120 us -> 114 us  [exchange(): pl.pallas_call(exchange_kernel, out_shape=(pltpu.VMEM((4, 8, 4, BLK, BLK)...]
    pallas_call x1, Pallas kernels: 10.2 us -> 8.23 us  [update(): pl.pallas_call(update_kernel, out_shape=(jax.ShapeDtypeStruct(front.shape...]
where the time goes in v3:
time: 124 us
  Pallas kernels  123 us (99%)
    pallas_call x1, Pallas kernels, exchange(): pl.pallas_call(exchange_kernel, out_shape=(pltpu.VMEM((4, 8, 4, BLK, BLK)...  114 us
    pallas_call x1, Pallas kernels, update(): pl.pallas_call(update_kernel, out_shape=(jax.ShapeDtypeStruct(front.shape...  8.23 us

profile of v3, /device:TPU:1, one launch (start us, length us, event | category | flops | bytes accessed | tf_op | source)
XLA Modules:
  0.0 124.0 jit_solution(6354537601103131098)
XLA Ops:
  0.6 114.5 %shard_map.59 = (bf16[4,8,4,128,128]{4,3,2,1,0:T(8,128)(2,1)S(1)}, bf16[4,2,128,512]{3,2,1,0:T(8,128)(2,1)S(1)}, bf16[4,2,2,128,512]{4,3,2,1,0:T(8,128)(2,1)S(1)}, f32[1024,2048]{1,0:T(8,128)S(1)}, s32[32]{0:T(128)}) custom-call(s32[2,64]{1,0:T(2,128)} %cm.1, bf16[8,128,1024]{2,1,0:T(8,128)(2,1)} %bitcast.4, f32[1024,2048]{1,0:T(8,128)} %front_hbm.1, ...), custom_call_target="tpu_custom_call" | custom-call | tf_op jit(solution)/shard_map/pallas_call | solution.py:445
  115.1 0.0 copy-start
  115.1 0.7 copy-done
  115.8 8.2 %shard_map.60 = (f32[1024,2048]{1,0:T(8,128)}, bf16[8,128,512]{2,1,0:T(8,128)(2,1)}) custom-call(s32[32]{0:T(128)S(1)} %copy-done, f32[1024,2048]{1,0:T(8,128)S(1)} %get-tuple-element.10.front, bf16[8,128,512]{2,1,0:T(8,128)(2,1)S(1)} %bitcast.3, bf16[4,2,2,128,512]{4,3,2,1,0:T(8,128)(2,1)S(1)} %get-tuple-element.12.cols, ...), custom_call_target="tpu_custom_call" | custom-call | tf_op jit(solution)/shard_map/pallas_call | solution.py:537
Async XLA Ops:
  115.1 0.7 copy-start

commit v4 on v3

--- a/solution.py
+++ b/solution.py
@@ -449,7 +449,7 @@
             pltpu.VMEM((4, 2, BLK, 4 * BLK), bf),
             pltpu.VMEM((4, 2, 2, BLK, 4 * BLK), bf),
             pltpu.VMEM(front.shape, f32),
-            jax.ShapeDtypeStruct((32,), jnp.int32),
+            pltpu.SMEM((32,), jnp.int32),
         ),
         in_specs=[smem, any_spec, any_spec, any_spec],
         out_specs=(any_spec, any_spec, any_spec, any_spec, smem),

time: 124 us -> 123 us (level)
  no operation moved by 1% of the time
where the time goes in v4:
time: 123 us; the launch traced here: 122 us
  Pallas kernels  122 us (99%)
    pallas_call x1, Pallas kernels, exchange(): pl.pallas_call(exchange_kernel, out_shape=(pltpu.VMEM((4, 8, 4, BLK, BLK)...  114 us
    pallas_call x1, Pallas kernels, update(): pl.pallas_call(update_kernel, out_shape=(jax.ShapeDtypeStruct(front.shape...  7.78 us

profile of v4, /device:TPU:1, one launch (start us, length us, event | category | flops | bytes accessed | tf_op | source)
XLA Modules:
  0.0 122.3 jit_solution(17024730687341025006)
XLA Ops:
  0.6 113.9 %shard_map.59 = (bf16[4,8,4,128,128]{4,3,2,1,0:T(8,128)(2,1)S(1)}, bf16[4,2,128,512]{3,2,1,0:T(8,128)(2,1)S(1)}, bf16[4,2,2,128,512]{4,3,2,1,0:T(8,128)(2,1)S(1)}, f32[1024,2048]{1,0:T(8,128)S(1)}, s32[32]{0:T(128)S(4)}) custom-call(s32[2,64]{1,0:T(2,128)} %cm.1, bf16[8,128,1024]{2,1,0:T(8,128)(2,1)} %bitcast.4, f32[1024,2048]{1,0:T(8,128)} %front_hbm.1, ...), custom_call_target="tpu_custom_call" | custom-call | tf_op jit(solution)/shard_map/pallas_call | solution.py:445
  114.6 7.8 %shard_map.60 = (f32[1024,2048]{1,0:T(8,128)}, bf16[8,128,512]{2,1,0:T(8,128)(2,1)}) custom-call(s32[32]{0:T(128)S(4)} %get-tuple-element.9.tab, f32[1024,2048]{1,0:T(8,128)S(1)} %get-tuple-element.10.front, bf16[8,128,512]{2,1,0:T(8,128)(2,1)S(1)} %bitcast.3, bf16[4,2,2,128,512]{4,3,2,1,0:T(8,128)(2,1)S(1)} %get-tuple-element.12.cols, ...), custom_call_target="tpu_custom_call" | custom-call | tf_op jit(solution)/shard_map/pallas_call | solution.py:537
